TPU v7x, 32 devices: a whole 2x2x4 slice. The times are simulated.
32 devices in a mesh: pair: 32 (over z, y, x, core), red: 1.
Axes of the slice: x: 2, y: 2, z: 4, core: 2. Of those that a mesh axis runs over, the one named last changes fastest.
Arguments:
- integrals: bfloat16 [256, 64, 1536], P(('pair', 'red')), may hold values from -6 to 6
- coeffs: bfloat16 [6016, 256], replicated, may hold values from -0.078125 to 0.078125
- shell_pairs: int32 [256, 2], replicated, may hold values from 0 to 93, as said below
- block_count: int32 [32, 1], P('pair', 'red'), may hold values from 1 to 8, as said below
Outputs:
- mo_ints: float32 [256, 24, 256], P('pair', None, 'red')
Inputs may be any that keep to these rules, and one draw needn't show every extreme that they name: `shell_pairs`: the 256 rows are distinct shell pairs (row shell, column shell). `block_count`: some device has all 8 slots live.
All inputs are finite; a program needn't handle non-finite values.
Results may differ from a plain program's by a relative error of at most 0.0029.
Values may be sent and summed in bfloat16 or wider, within the bound.
A program may use at most 128 MiB of HBM per device.

v0:
```python
import jax
import jax.numpy as jnp
from jax import lax
from jax.sharding import PartitionSpec as P


def on_device(integrals, coeffs, shell_pairs, block_count):
    slot_count = integrals.shape[0]
    shell_size = integrals.shape[1]
    ket_count = integrals.shape[2] // shell_size
    occ_count = coeffs.shape[1]
    shell_count = coeffs.shape[0] // shell_size
    pair_count = lax.axis_size("pair")
    red_count = lax.axis_size("red")
    pair_index = lax.axis_index("pair")
    red_index = lax.axis_index("red")
    owned_rows = occ_count // pair_count
    coef_table = coeffs.reshape(shell_count, shell_size, occ_count)
    first_slot = (pair_index * red_count + red_index) * slot_count
    own_pairs = lax.dynamic_slice_in_dim(shell_pairs, first_slot, slot_count, 0)
    live_mask = (jnp.arange(slot_count, dtype=jnp.int32) < block_count[0, 0]).astype(jnp.float32)
    left_panels = jnp.take(coef_table, own_pairs[:, 0], axis=0)
    half_done = jnp.einsum(
        "kmi,kmx->kix", left_panels, integrals, preferred_element_type=jnp.float32
    )
    half_done = (half_done * live_mask[:, None, None]).astype(jnp.bfloat16)
    right_panels = jnp.take(coef_table, own_pairs[:, 1], axis=0)
    whole_sum = jnp.einsum(
        "kpiqn,knrj->priqj",
        half_done.reshape(slot_count, pair_count, owned_rows, ket_count, shell_size),
        right_panels.reshape(slot_count, shell_size, red_count, occ_count // red_count),
        preferred_element_type=jnp.float32,
    )
    whole_sum = whole_sum.reshape(
        pair_count * red_count * owned_rows, ket_count, occ_count // red_count
    )
    return lax.psum_scatter(whole_sum, ("pair", "red"), scatter_dimension=0, tiled=True)


def solution(mesh):
    return jax.shard_map(
        on_device,
        mesh=mesh,
        in_specs=(P(("pair", "red"), None, None), P(), P(), P("pair", "red")),
        out_specs=P("pair", None, "red"),
        check_vma=False,
    )
```

profile of v0, /device:TPU:0, one launch (start us, length us, event | category | flops | bytes accessed | tf_op | source)
XLA Modules:
  0.0 181.7 jit_solution(11172767026649673448)
XLA Ops:
  6.5 0.0 copy-start
  6.5 0.0 reduce-scatter.2.cloned.1.call-start
  7.4 0.9 constant_dynamic-slice_fusion
  8.3 0.2 copy-done
  8.4 0.6 gather_fusion.1
  9.0 1.3 gather_fusion
  10.3 6.2 %multiply_convert_fusion = bf16[8,256,1536]{2,1,0:T(8,128)(2,1)} fusion(bf16[8,64,1536]{2,1,0:T(8,128)(2,1)} %param.6, f32[8]{0:T(128)S(1)} %compare_convert_fusion, bf16[8,64,256]{2,1,0:T(8,128)(2,1)S(1)} %gather_fusion.1, pred[8]{0:T(512)(128)(4,1)S(1)} %get-tuple-element.10), kind=kOutput, calls=%fused_computation.4 | convolution fusion | flops 409075712 | bytes 8126504 | tf_op jit(solution)/shard_map/kmi,kmx->kix/dot_general | solution.py:23
  16.5 0.0 copy-start.1
  16.5 16.3 %reshape.24 = bf16[8,32,8,24,64]{4,3,2,1,0:T(8,128)(2,1)} reshape(bf16[8,256,1536]{2,1,0:T(8,128)(2,1)} %multiply_convert_fusion) | data formatting | bytes 12582912 | tf_op jit(solution)/shard_map/reshape | solution.py:30
  32.8 0.0 copy-done.1
  32.8 18.3 %fusion.2 = f32[32,1,8,24,256]{4,0,3,2,1:T(8,128)S(1)} fusion(bf16[8,32,8,24,64]{4,3,2,1,0:T(8,128)(2,1)} %reshape.24, bf16[8,64,256]{2,1,0:T(8,128)(2,1)S(1)} %copy-done.1, pred[8]{0:T(512)(128)(4,1)S(1)} %get-tuple-element.6), kind=kOutput, calls=%fused_computation.5 | convolution fusion | flops 1610743808 | bytes 12845064 | tf_op jit(solution)/shard_map/kpiqn,knrj->priqj/dot_general | solution.py:28
  51.0 6.3 %copy.7 = f32[32,1,8,24,256]{4,3,2,0,1:T(8,128)} copy(f32[32,1,8,24,256]{4,0,3,2,1:T(8,128)S(1)} %fusion.2) | data formatting | bytes 12582912 | tf_op jit(solution)/shard_map/kpiqn,knrj->priqj/transpose | solution.py:28
  57.3 0.0 reduce-scatter.2.cloned.1.call-update
  57.4 117.5 %reduce-scatter.2.cloned.1.call-done = f32[8,24,256]{2,1,0:T(8,128)} async-done(((f32[256,24,256]{2,1,0:T(8,128)}), f32[8,24,256]{2,1,0:T(8,128)}) %reduce-scatter.2.cloned.1.call-update) | async-done | bytes 196624 | tf_op jit(solution)/shard_map/reduce_scatter | solution.py:37
  (3 shorter events, 0.0 us)
Async XLA Ops:
  6.5 1.9 %copy-start = (bf16[6016,256]{1,0:T(8,128)(2,1)S(1)}, bf16[6016,256]{1,0:T(8,128)(2,1)}, u32[]{:S(2)}) copy-start(bf16[6016,256]{1,0:T(8,128)(2,1)} %param.7) | copy-start | bytes 9240580
  6.5 168.3 %reduce-scatter.2.cloned.1.call-start = ((), (), s32[]{:S(2)}) async-start(), calls=%async_computation.1 | async-start | bytes 6488064 | tf_op jit(solution)/shard_map/reduce_scatter | solution.py:37
  16.5 16.3 %copy-start.1 = (bf16[8,64,256]{2,1,0:T(8,128)(2,1)S(1)}, bf16[8,64,256]{2,1,0:T(8,128)(2,1)}, u32[]{:S(2)}) copy-start(bf16[8,64,256]{2,1,0:T(8,128)(2,1)} %gather_fusion) | copy-start | bytes 786436
Sparse Core Ops, SparseCore 0:
  57.5 117.3 reduce-scatter.1
where the time goes:
time: 182 us
  waiting for transfers between devices  118 us (65%)
  local copies, waits for them, and re-layouts  25.5 us (14%)
  matrix products  24.5 us (13%)
  between operations  14.2 us (8%)
    reduce_scatter x1, waiting for transfers between devices, on_device(): lax.psum_scatter(whole_sum, ('pair', 'red'), scatter_dimension=0, tiled=T...  117 us
    dot_general x1, matrix products, on_device(): jnp.einsum('kpiqn,knrj->priqj', half_done.reshape(slot_count, pair_count,...  18.3 us
    reshape x1, local copies, waits for them, and re-layouts, on_device(): half_done.reshape(slot_count, pair_count, owned_rows, ket_count, shell_size)  16.3 us
    transpose x1, local copies, waits for them, and re-layouts, on_device(): jnp.einsum('kpiqn,knrj->priqj', half_done.reshape(slot_count, pair_count,...  6.29 us
    dot_general x1, matrix products, on_device(): jnp.einsum('kmi,kmx->kix', left_panels, integrals, preferred_element_type...  6.21 us
  transfers between devices with their start and end apart: 1, of which 1 were waited for; matrix products, arithmetic and copies ran while one was open for 0% of the time, Pallas kernels for 0%

commit v1 on v0

--- a/solution.py
+++ b/solution.py
@@ -1,10 +1,251 @@
+import functools
+import math
+
 import jax
 import jax.numpy as jnp
 from jax import lax
+from jax.experimental import pallas as pl
+from jax.experimental.pallas import tpu as pltpu
 from jax.sharding import PartitionSpec as P
 
+GROUPS = 6
+LOW_EXP = -80.0
+
+
+def encode(x, steps):
+    level = jnp.log(jnp.abs(x)) * (steps / math.log(2.0)) + (0.5 - LOW_EXP * steps)
+    code = jnp.clip(level, 0.0, 32767.0).astype(jnp.int32)
+    return jnp.where(x < 0.0, -code, code).astype(jnp.int16)
+
+
+def decode(code, steps):
+    wide = code.astype(jnp.int32).astype(jnp.float32)
+    size = jnp.exp2(jnp.abs(wide) * (1.0 / steps) + LOW_EXP)
+    value = jnp.where(wide < 0.0, -size, size)
+    return jnp.where(wide == 0.0, 0.0, value)
+
+
+def transform_kernel(
+    steps,
+    pairs_ref, count_ref, coeffs_hbm, ints_hbm, out_ref,
+    coeffs, ints, turned, left, right, diag,
+    own, snd0, rcv0, snd1, rcv1, snd2, rcv2, snd3, rcv3,
+    load_sem, send_sem, recv_sem,
+):
+    load_coeffs = pltpu.make_async_copy(coeffs_hbm, coeffs, load_sem.at[0])
+    load_ints = pltpu.make_async_copy(ints_hbm, ints, load_sem.at[1])
+    load_coeffs.start()
+    load_ints.start()
+
+    me = lax.axis_index("pair")
+
+    def other(bit):
+        return me + bit * (1 - 2 * ((me // bit) % 2))
+
+    core_at, x_at, y_at = other(1), other(2), other(4)
+    z_low, z_high = other(8) - me, other(16) - me
+    z_at = (me + z_low, me + z_high, me + z_low + z_high)
+    partners = (core_at, x_at, y_at) + z_at
+
+    barrier = pltpu.get_barrier_semaphore()
+    for at in partners:
+        pl.semaphore_signal(
+            barrier, inc=1, device_id={"pair": at}, device_id_type=pl.DeviceIdType.MESH
+        )
+
+    slots, width, columns = ints.shape
+    occ = coeffs.shape[2]
+    span = 4 * width
+    diag[...] = jnp.zeros_like(diag)
+    load_coeffs.wait()
+    for k in range(slots):
+        row_shell = pairs_ref[me * slots + k, 0]
+        col_shell = pairs_ref[me * slots + k, 1]
+        live = jnp.where(k < count_ref[0, 0], 1.0, 0.0).astype(jnp.float32)
+        panel = coeffs[row_shell].astype(jnp.float32) * live
+        turned[k // 4, :, :, pl.ds((k % 4) * width, width)] = panel.T.reshape(
+            occ // 8, 8, width
+        )
+        right[pl.ds(k * width, width), :] = coeffs[col_shell]
+
+    bits = [(me // w) % 2 for w in (1, 2, 4, 8, 16)]
+
+    def place(rel):
+        return sum(((rel // w) % 2 + b - 2 * ((rel // w) % 2) * b) * w
+                   for w, b in zip((1, 2, 4, 8, 16), bits))
+
+    for core in range(2):
+        for two in range(8):
+            first = place(core + 2 * (2 * two))
+            second = place(core + 2 * (2 * two + 1))
+            for part in range(2):
+                rows = jnp.concatenate([turned[part, first], turned[part, second]], axis=0)
+                left[part, pl.ds(core * 128 + two * 16, 16), :] = rows.astype(jnp.bfloat16)
+
+    load_ints.wait()
+
+    lane = lax.broadcasted_iota(jnp.int32, (width, 2 * width), 1)
+    low = lane < width
+    per_group = columns // (2 * width) // GROUPS
+
+    def compute(group):
+        def one_pair(step, carry):
+            cols = pl.ds(pl.multiple_of((group * per_group + step) * 2 * width, 2 * width), 2 * width)
+            for k in range(slots):
+                tile = ints[k, :, cols].astype(jnp.float32)
+                swap = pltpu.roll(tile, width, 1)
+                at_lane = pl.ds((k % 4) // 2 * 2 * width, 2 * width)
+                at_row = pl.ds((k % 4) * width, width)
+                for odd in range(2):
+                    source = tile if k % 2 == odd else swap
+                    keep = low if k % 2 == 0 else jnp.logical_not(low)
+                    diag[odd, k // 4, at_row, at_lane] = jnp.where(keep, source, 0.0).astype(jnp.bfloat16)
+            done = []
+            for odd in range(2):
+                half = jnp.concatenate(
+                    [
+                        jnp.dot(left[part], diag[odd, part], preferred_element_type=jnp.float32).astype(jnp.bfloat16)
+                        for part in range(2)
+                    ],
+                    axis=1,
+                )
+                done.append(jnp.dot(half, right[...], preferred_element_type=jnp.float32).reshape(2, 4, 2, 2, 8, occ))
+            both = jnp.concatenate(done, axis=4)
+            own[group, :, :, :, step] = both[0]
+            snd0[group, :, :, :, step] = both[1].astype(jnp.bfloat16)
+            return carry
+
+        lax.fori_loop(0, per_group, one_pair, 0)
+
+    def copy(group, stage, source, target, at):
+        return pltpu.make_async_remote_copy(
+            src_ref=source,
+            dst_ref=target,
+            send_sem=send_sem.at[group, stage],
+            recv_sem=recv_sem.at[group, stage],
+            device_id={"pair": at},
+            device_id_type=pl.DeviceIdType.MESH,
+        )
+
+    def copies(group):
+        first, second = (x_at, y_at) if group % 2 == 0 else (y_at, x_at)
+        made = [
+            copy(group, 0, snd0.at[group], rcv0.at[group], core_at),
+            copy(group, 1, snd1.at[group], rcv1.at[group], first),
+            copy(group, 2, snd2.at[group], rcv2.at[group], second),
+        ]
+        for n in range(3):
+            made.append(copy(group, 3 + n, snd3.at[group, n], rcv3.at[group, n], z_at[n]))
+        return made
+
+    plan = [copies(group) for group in range(GROUPS)]
+
+    def chunk(group, z, a, b):
+        y, x = (a, b) if group % 2 == 0 else (b, a)
+        return own[group, z, y, x] + rcv0[group, z, y, x].astype(jnp.float32)
+
+    def stage1(group):
+        plan[group][0].wait_recv()
+
+        def body(z, carry):
+            for a in range(2):
+                snd1[group, z, a] = encode(chunk(group, z, a, 1), steps)
+            return carry
+
+        lax.fori_loop(0, 4, body, 0)
+        plan[group][1].start()
+
+    def stage2(group):
+        plan[group][1].wait_recv()
+
+        def body(z, carry):
+            total = chunk(group, z, 1, 0) + decode(rcv1[group, z, 1], steps)
+            snd2[group, z] = encode(total, steps)
+            return carry
+
+        lax.fori_loop(0, 4, body, 0)
+        plan[group][2].start()
+
+    def gathered(group, z):
+        return (
+            chunk(group, z, 0, 0)
+            + decode(rcv1[group, z, 0], steps)
+            + decode(rcv2[group, z], steps)
+        )
+
+    def stage3(group):
+        plan[group][2].wait_recv()
+        for n in (1, 2, 0):
+            snd3[group, n] = encode(gathered(group, n + 1), steps)
+            plan[group][3 + n].start()
+
+    def finish(group):
+        total = gathered(group, 0)
+        for n in range(3):
+            plan[group][3 + n].wait_recv()
+            total = total + decode(rcv3[group, n], steps)
+        out_ref[group] = total
+
+    stages = (stage1, stage2, stage3, finish)
+    for tick in range(GROUPS + len(stages)):
+        if tick < GROUPS:
+            compute(tick)
+            if tick == 0:
+                pl.semaphore_wait(barrier, len(partners))
+            plan[tick][0].start()
+        for later, stage in enumerate(stages):
+            if 0 <= tick - 1 - later < GROUPS:
+                stage(tick - 1 - later)
+    for group in range(GROUPS):
+        for item in plan[group]:
+            item.wait_send()
+
 
 def on_device(integrals, coeffs, shell_pairs, block_count):
+    slots, width, columns = integrals.shape
+    occ = coeffs.shape[1]
+    kets = columns // width
+    shells = coeffs.shape[0] // width
+    per_group = kets // 2 // GROUPS
+    top = math.ceil(math.log2(shell_pairs.shape[0] * width * width * 6 * 0.078125 ** 2)) + 1
+    steps = 32760.0 / (top - LOW_EXP)
+    tile = (per_group, 16, occ)
+    bf16, i16 = jnp.bfloat16, jnp.int16
+    hbm = pl.BlockSpec(memory_space=pl.ANY)
+    smem = pl.BlockSpec(memory_space=pltpu.SMEM)
+    out = pl.pallas_call(
+        functools.partial(transform_kernel, steps),
+        out_shape=jax.ShapeDtypeStruct((GROUPS,) + tile, jnp.float32),
+        in_specs=[smem, smem, hbm, hbm],
+        out_specs=pl.BlockSpec(memory_space=pltpu.VMEM),
+        scratch_shapes=[
+            pltpu.VMEM((shells, width, occ), bf16),
+            pltpu.VMEM(integrals.shape, bf16),
+            pltpu.VMEM((2, occ // 8, 8, 4 * width), jnp.float32),
+            pltpu.VMEM((2, occ, 4 * width), bf16),
+            pltpu.VMEM((slots * width, occ), bf16),
+            pltpu.VMEM((2, 2, 4 * width, 4 * width), bf16),
+            pltpu.VMEM((GROUPS, 4, 2, 2) + tile, jnp.float32),
+            pltpu.VMEM((GROUPS, 4, 2, 2) + tile, bf16),
+            pltpu.VMEM((GROUPS, 4, 2, 2) + tile, bf16),
+            pltpu.VMEM((GROUPS, 4, 2) + tile, i16),
+            pltpu.VMEM((GROUPS, 4, 2) + tile, i16),
+            pltpu.VMEM((GROUPS, 4) + tile, i16),
+            pltpu.VMEM((GROUPS, 4) + tile, i16),
+            pltpu.VMEM((GROUPS, 3) + tile, i16),
+            pltpu.VMEM((GROUPS, 3) + tile, i16),
+            pltpu.SemaphoreType.DMA((2,)),
+            pltpu.SemaphoreType.DMA((GROUPS, 6)),
+            pltpu.SemaphoreType.DMA((GROUPS, 6)),
+        ],
+        compiler_params=pltpu.CompilerParams(
+            collective_id=0, has_side_effects=True, vmem_limit_bytes=48 * 1024 * 1024
+        ),
+    )(shell_pairs, block_count, coeffs.reshape(shells, width, occ), integrals)
+    return out.reshape(kets, occ // 32, occ).transpose(1, 0, 2)
+
+
+def on_device_general(integrals, coeffs, shell_pairs, block_count):
     slot_count = integrals.shape[0]
     shell_size = integrals.shape[1]
     ket_count = integrals.shape[2] // shell_size
@@ -38,8 +279,9 @@
 
 
 def solution(mesh):
+    small = mesh.shape["pair"] == 32 and mesh.shape["red"] == 1
     return jax.shard_map(
-        on_device,
+        on_device if small else on_device_general,
         mesh=mesh,
         in_specs=(P(("pair", "red"), None, None), P(), P(), P("pair", "red")),
         out_specs=P("pair", None, "red"),

time: 182 us -> 45.3 us (0.25)
  waiting for transfers between devices: 118 us -> 0 us
  Pallas kernels: 0 us -> 39.6 us
  matrix products: 24.5 us -> 0 us
  local copies, waits for them, and re-layouts: 25.5 us -> 4.82 us
  between operations: 14.2 us -> 0.68 us
    reduce_scatter x1 -> x0, waiting for transfers between devices: 117 us -> none  [on_device(): lax.psum_scatter(whole_sum, ('pair', 'red'), scatter_dimension=0, tiled=T...]
    pallas_call x0 -> x1, Pallas kernels: none -> 39.6 us  [on_device(): pl.pallas_call(functools.partial(transform_kernel, steps), out_shape=jax....]
    dot_general x2 -> x0, matrix products: 24.5 us -> none  [the longest x1 18.3 us: on_device(): jnp.einsum('kpiqn,knrj->priqj', half_done.reshape(slot_count, pair_count,...]
    reshape x1, local copies, waits for them, and re-layouts: 16.3 us -> 0.74 us  [on_device(): return out.reshape(kets, occ // 32, occ).transpose(1, 0, 2)]
    transpose x1 -> x0, local copies, waits for them, and re-layouts: 6.29 us -> none  [on_device(): jnp.einsum('kpiqn,knrj->priqj', half_done.reshape(slot_count, pair_count,...]
    unnamed x4 -> x5, local copies, waits for them, and re-layouts: 0.17 us -> 4.08 us
    gather x2 -> x0, local copies, waits for them, and re-layouts: 1.83 us -> none  [the longest x1 1.27 us: on_device(): right_panels = jnp.take(coef_table, own_pairs[:, 1], axis=0)]
  transfers between devices with their start and end apart: 1 -> 0, of which waited for: 1 -> 0; matrix products, arithmetic and copies ran while one was open for 0% -> 0% of each run, Pallas kernels for 0% -> 0%
where the time goes in v1:
time: 45.3 us; the launch traced here: 45.1 us
  Pallas kernels  39.6 us (87%)
  local copies, waits for them, and re-layouts  4.82 us (11%)
  between operations  0.68 us (2%)
    pallas_call x1, Pallas kernels, on_device(): pl.pallas_call(functools.partial(transform_kernel, steps), out_shape=jax....  39.6 us
    unnamed x5, local copies, waits for them, and re-layouts  4.08 us

profile of v1, /device:TPU:0, one launch (start us, length us, event | category | flops | bytes accessed | tf_op | source)
XLA Modules:
  0.0 45.1 jit_solution(12557169535453313361)
XLA Ops:
  0.7 0.8 %copy.5.pairs_ref = s32[256,2]{1,0:T(8,128)S(1)} copy(s32[256,2]{0,1:T(2,128)} %param.6) | data formatting | bytes 4096 | tf_op args[2]
  1.5 0.0 copy-start
  1.5 1.9 %copy-done = bf16[6016,256]{1,0:T(8,128)(2,1)S(1)} copy-done((bf16[6016,256]{1,0:T(8,128)(2,1)S(1)}, bf16[6016,256]{1,0:T(8,128)(2,1)}, u32[]{:S(2)}) %copy-start) | copy-done | bytes 3080216
  3.3 0.0 copy-start.1
  3.3 1.4 %copy-done.1 = bf16[8,64,1536]{2,1,0:T(8,128)(2,1)S(1)} copy-done((bf16[8,64,1536]{2,1,0:T(8,128)(2,1)S(1)}, bf16[8,64,1536]{2,1,0:T(8,128)(2,1)}, u32[]{:S(2)}) %copy-start.1) | copy-done | bytes 1572888
  4.8 39.6 %shard_map.46 = f32[6,2,16,256]{3,2,1,0:T(8,128)S(1)} custom-call(s32[256,2]{1,0:T(8,128)S(1)} %copy.5.pairs_ref, s32[1,1]{1,0:T(1,128)S(6)} %copy.9.count_ref, bf16[94,64,256]{2,1,0:T(8,128)(2,1)S(1)} %bitcast.5, bf16[8,64,1536]{2,1,0:T(8,128)(2,1)S(1)} %copy-done.1), custom_call_target="tpu_custom_call" | custom-call | tf_op jit(solution)/shard_map/pallas_call | solution.py:216
  44.4 0.7 %copy.8 = f32[24,8,256]{2,0,1:T(8,128)} copy(f32[24,8,256]{2,1,0:T(8,128)S(1)} %bitcast.6) | data formatting | bytes 393216 | tf_op jit(solution)/shard_map/reshape | solution.py:245
Async XLA Ops:
  1.5 1.9 %copy-start = (bf16[6016,256]{1,0:T(8,128)(2,1)S(1)}, bf16[6016,256]{1,0:T(8,128)(2,1)}, u32[]{:S(2)}) copy-start(bf16[6016,256]{1,0:T(8,128)(2,1)} %param.5) | copy-start | bytes 9240580
  3.3 1.4 %copy-start.1 = (bf16[8,64,1536]{2,1,0:T(8,128)(2,1)S(1)}, bf16[8,64,1536]{2,1,0:T(8,128)(2,1)}, u32[]{:S(2)}) copy-start(bf16[8,64,1536]{2,1,0:T(8,128)(2,1)} %ints_hbm.1) | copy-start | bytes 4718596

commit v2 on v1

--- a/solution.py
+++ b/solution.py
@@ -8,14 +8,15 @@
 from jax.experimental.pallas import tpu as pltpu
 from jax.sharding import PartitionSpec as P
 
-GROUPS = 6
+GROUPS = 12
+LAGS = (1, 3, 5, 7)
 LOW_EXP = -80.0
 
 
 def encode(x, steps):
     level = jnp.log(jnp.abs(x)) * (steps / math.log(2.0)) + (0.5 - LOW_EXP * steps)
-    code = jnp.clip(level, 0.0, 32767.0).astype(jnp.int32)
-    return jnp.where(x < 0.0, -code, code).astype(jnp.int16)
+    level = jnp.maximum(level, 0.0)
+    return jnp.where(x < 0.0, -level, level).astype(jnp.int32).astype(jnp.int16)
 
 
 def decode(code, steps):
@@ -59,8 +60,8 @@
     diag[...] = jnp.zeros_like(diag)
     load_coeffs.wait()
     for k in range(slots):
-        row_shell = pairs_ref[me * slots + k, 0]
-        col_shell = pairs_ref[me * slots + k, 1]
+        row_shell = pairs_ref[0, me * slots + k]
+        col_shell = pairs_ref[1, me * slots + k]
         live = jnp.where(k < count_ref[0, 0], 1.0, 0.0).astype(jnp.float32)
         panel = coeffs[row_shell].astype(jnp.float32) * live
         turned[k // 4, :, :, pl.ds((k % 4) * width, width)] = panel.T.reshape(
@@ -127,78 +128,91 @@
             device_id_type=pl.DeviceIdType.MESH,
         )
 
-    def copies(group):
-        first, second = (x_at, y_at) if group % 2 == 0 else (y_at, x_at)
-        made = [
-            copy(group, 0, snd0.at[group], rcv0.at[group], core_at),
-            copy(group, 1, snd1.at[group], rcv1.at[group], first),
-            copy(group, 2, snd2.at[group], rcv2.at[group], second),
-        ]
-        for n in range(3):
-            made.append(copy(group, 3 + n, snd3.at[group, n], rcv3.at[group, n], z_at[n]))
-        return made
-
-    plan = [copies(group) for group in range(GROUPS)]
-
-    def chunk(group, z, a, b):
-        y, x = (a, b) if group % 2 == 0 else (b, a)
+    def core_copy(group):
+        return copy(group, 0, snd0.at[group], rcv0.at[group], core_at)
+
+    def first_copy(group, kind):
+        at = y_at if kind else x_at
+        return copy(group, 1, snd1.at[group], rcv1.at[group], at)
+
+    def second_copy(group, kind):
+        at = x_at if kind else y_at
+        return copy(group, 2, snd2.at[group], rcv2.at[group], at)
+
+    def z_copy(group, n):
+        return copy(group, 3 + n, snd3.at[group, n], rcv3.at[group, n], z_at[n])
+
+    def chunks(group, kind, z, a, b):
+        y, x = (a, b) if kind == 0 else (b, a)
         return own[group, z, y, x] + rcv0[group, z, y, x].astype(jnp.float32)
 
-    def stage1(group):
-        plan[group][0].wait_recv()
-
-        def body(z, carry):
-            for a in range(2):
-                snd1[group, z, a] = encode(chunk(group, z, a, 1), steps)
-            return carry
-
-        lax.fori_loop(0, 4, body, 0)
-        plan[group][1].start()
-
-    def stage2(group):
-        plan[group][1].wait_recv()
-
-        def body(z, carry):
-            total = chunk(group, z, 1, 0) + decode(rcv1[group, z, 1], steps)
-            snd2[group, z] = encode(total, steps)
-            return carry
-
-        lax.fori_loop(0, 4, body, 0)
-        plan[group][2].start()
-
-    def gathered(group, z):
+    def stage1(group, kind):
+        core_copy(group).wait_recv()
+        snd1[group] = encode(chunks(group, kind, slice(None), slice(None), 1), steps)
+        first_copy(group, kind).start()
+
+    def stage2(group, kind):
+        first_copy(group, kind).wait_recv()
+        total = chunks(group, kind, slice(None), 1, 0) + decode(rcv1[group, :, 1], steps)
+        snd2[group] = encode(total, steps)
+        second_copy(group, kind).start()
+
+    def gathered(group, kind, z):
         return (
-            chunk(group, z, 0, 0)
+            chunks(group, kind, z, 0, 0)
             + decode(rcv1[group, z, 0], steps)
             + decode(rcv2[group, z], steps)
         )
 
-    def stage3(group):
-        plan[group][2].wait_recv()
+    def stage3(group, kind):
+        second_copy(group, kind).wait_recv()
         for n in (1, 2, 0):
-            snd3[group, n] = encode(gathered(group, n + 1), steps)
-            plan[group][3 + n].start()
-
-    def finish(group):
-        total = gathered(group, 0)
+            snd3[group, n] = encode(gathered(group, kind, n + 1), steps)
+            z_copy(group, n).start()
+
+    def finish(group, kind):
+        total = gathered(group, kind, 0)
         for n in range(3):
-            plan[group][3 + n].wait_recv()
-            total = total + decode(rcv3[group, n], steps)
+            z_copy(group, n).wait_recv()
+        total = total + jnp.sum(decode(rcv3[group], steps), axis=0)
         out_ref[group] = total
 
     stages = (stage1, stage2, stage3, finish)
-    for tick in range(GROUPS + len(stages)):
-        if tick < GROUPS:
-            compute(tick)
-            if tick == 0:
-                pl.semaphore_wait(barrier, len(partners))
-            plan[tick][0].start()
-        for later, stage in enumerate(stages):
-            if 0 <= tick - 1 - later < GROUPS:
-                stage(tick - 1 - later)
-    for group in range(GROUPS):
-        for item in plan[group]:
-            item.wait_send()
+
+    def two_ticks(turn, carry):
+        for kind in range(2):
+            tick = 2 * turn + kind
+
+            @pl.when(tick < GROUPS)
+            def _():
+                compute(tick)
+                if kind == 0:
+                    @pl.when(turn == 0)
+                    def _():
+                        pl.semaphore_wait(barrier, len(partners))
+                core_copy(tick).start()
+
+            for lag, stage in zip(LAGS, stages):
+                group = tick - lag
+
+                @pl.when(jnp.logical_and(group >= 0, group < GROUPS))
+                def _(group=group, stage=stage):
+                    stage(group, 1 - kind)
+        return carry
+
+    lax.fori_loop(0, (GROUPS + LAGS[-1] + 1) // 2, two_ticks, 0)
+
+    def drain(half, carry):
+        for kind in range(2):
+            group = 2 * half + kind
+            core_copy(group).wait_send()
+            first_copy(group, kind).wait_send()
+            second_copy(group, kind).wait_send()
+            for n in range(3):
+                z_copy(group, n).wait_send()
+        return carry
+
+    lax.fori_loop(0, GROUPS // 2, drain, 0)
 
 
 def on_device(integrals, coeffs, shell_pairs, block_count):
@@ -239,9 +253,9 @@
             pltpu.SemaphoreType.DMA((GROUPS, 6)),
         ],
         compiler_params=pltpu.CompilerParams(
-            collective_id=0, has_side_effects=True, vmem_limit_bytes=48 * 1024 * 1024
+            collective_id=0, has_side_effects=True, vmem_limit_bytes=60 * 1024 * 1024
         ),
-    )(shell_pairs, block_count, coeffs.reshape(shells, width, occ), integrals)
+    )(shell_pairs.T, block_count, coeffs.reshape(shells, width, occ), integrals)
     return out.reshape(kets, occ // 32, occ).transpose(1, 0, 2)
 
 

time: 45.3 us -> 40.6 us (0.90)
  local copies, waits for them, and re-layouts: 4.82 us -> 1.67 us
  Pallas kernels: 39.6 us -> 38.1 us
    unnamed x5 -> x0, local copies, waits for them, and re-layouts: 4.08 us -> none
    pallas_call x1, Pallas kernels: 39.6 us -> 38.1 us  [on_device(): pl.pallas_call(functools.partial(transform_kernel, steps), out_shape=jax....]
    reshape x1, local copies, waits for them, and re-layouts: 0.74 us -> 1.67 us  [on_device(): return out.reshape(kets, occ // 32, occ).transpose(1, 0, 2)]
where the time goes in v2:
time: 40.6 us; the launch traced here: 40.4 us
  Pallas kernels  38.1 us (94%)
  local copies, waits for them, and re-layouts  1.67 us (4%)
  between operations  0.66 us (2%)
    pallas_call x1, Pallas kernels, on_device(): pl.pallas_call(functools.partial(transform_kernel, steps), out_shape=jax....  38.1 us
    reshape x1, local copies, waits for them, and re-layouts, on_device(): return out.reshape(kets, occ // 32, occ).transpose(1, 0, 2)  1.67 us

profile of v2, /device:TPU:0, one launch (start us, length us, event | category | flops | bytes accessed | tf_op | source)
XLA Modules:
  0.0 40.4 jit_solution(17043319719473246782)
XLA Ops:
  0.7 38.1 %shard_map.46 = f32[12,1,16,256]{3,2,1,0:T(8,128)} custom-call(s32[2,256]{1,0:T(2,128)} %bitcast.8, s32[1,1]{1,0:T(1,128)S(6)} %copy.8.count_ref, bf16[94,64,256]{2,1,0:T(8,128)(2,1)} %bitcast.6, bf16[8,64,1536]{2,1,0:T(8,128)(2,1)} %ints_hbm.1), custom_call_target="tpu_custom_call" | custom-call | tf_op jit(solution)/shard_map/pallas_call | solution.py:230
  38.7 1.7 %copy.7 = f32[24,8,256]{2,0,1:T(8,128)} copy(f32[24,8,256]{2,1,0:T(8,128)} %bitcast.7) | data formatting | bytes 393216 | tf_op jit(solution)/shard_map/reshape | solution.py:259

commit v3 on v2

--- a/solution.py
+++ b/solution.py
@@ -9,7 +9,7 @@
 from jax.sharding import PartitionSpec as P
 
 GROUPS = 12
-LAGS = (1, 3, 5, 7)
+LAGS = (1, 5, 9, 13)
 LOW_EXP = -80.0
 
 
@@ -69,11 +69,14 @@
         )
         right[pl.ds(k * width, width), :] = coeffs[col_shell]
 
-    bits = [(me // w) % 2 for w in (1, 2, 4, 8, 16)]
+    moves = [other(w) - me for w in (1, 2, 4, 8, 16)]
 
     def place(rel):
-        return sum(((rel // w) % 2 + b - 2 * ((rel // w) % 2) * b) * w
-                   for w, b in zip((1, 2, 4, 8, 16), bits))
+        at = me
+        for n, move in enumerate(moves):
+            if (rel >> n) % 2:
+                at = at + move
+        return at
 
     for core in range(2):
         for two in range(8):
@@ -148,19 +151,19 @@
 
     def stage1(group, kind):
         core_copy(group).wait_recv()
-        snd1[group] = encode(chunks(group, kind, slice(None), slice(None), 1), steps)
+        snd1[group] = chunks(group, kind, slice(None), slice(None), 1).astype(jnp.bfloat16)
         first_copy(group, kind).start()
 
     def stage2(group, kind):
         first_copy(group, kind).wait_recv()
-        total = chunks(group, kind, slice(None), 1, 0) + decode(rcv1[group, :, 1], steps)
+        total = chunks(group, kind, slice(None), 1, 0) + rcv1[group, :, 1].astype(jnp.float32)
         snd2[group] = encode(total, steps)
         second_copy(group, kind).start()
 
     def gathered(group, kind, z):
         return (
             chunks(group, kind, z, 0, 0)
-            + decode(rcv1[group, z, 0], steps)
+            + rcv1[group, z, 0].astype(jnp.float32)
             + decode(rcv2[group, z], steps)
         )
 
@@ -242,8 +245,8 @@
             pltpu.VMEM((GROUPS, 4, 2, 2) + tile, jnp.float32),
             pltpu.VMEM((GROUPS, 4, 2, 2) + tile, bf16),
             pltpu.VMEM((GROUPS, 4, 2, 2) + tile, bf16),
-            pltpu.VMEM((GROUPS, 4, 2) + tile, i16),
-            pltpu.VMEM((GROUPS, 4, 2) + tile, i16),
+            pltpu.VMEM((GROUPS, 4, 2) + tile, bf16),
+            pltpu.VMEM((GROUPS, 4, 2) + tile, bf16),
             pltpu.VMEM((GROUPS, 4) + tile, i16),
             pltpu.VMEM((GROUPS, 4) + tile, i16),
             pltpu.VMEM((GROUPS, 3) + tile, i16),

time: 40.6 us -> 34.4 us (0.85)
  Pallas kernels: 38.1 us -> 31.9 us
    pallas_call x1, Pallas kernels: 38.1 us -> 31.9 us  [on_device(): pl.pallas_call(functools.partial(transform_kernel, steps), out_shape=jax....]
where the time goes in v3:
time: 34.4 us; the launch traced here: 34.3 us
  Pallas kernels  31.9 us (93%)
  local copies, waits for them, and re-layouts  1.67 us (5%)
  between operations  0.66 us (2%)
    pallas_call x1, Pallas kernels, on_device(): pl.pallas_call(functools.partial(transform_kernel, steps), out_shape=jax....  31.9 us
    reshape x1, local copies, waits for them, and re-layouts, on_device(): return out.reshape(kets, occ // 32, occ).transpose(1, 0, 2)  1.67 us

profile of v3, /device:TPU:0, one launch (start us, length us, event | category | flops | bytes accessed | tf_op | source)
XLA Modules:
  0.0 34.3 jit_solution(4798296752895900671)
XLA Ops:
  0.7 31.9 %shard_map.46 = f32[12,1,16,256]{3,2,1,0:T(8,128)} custom-call(s32[2,256]{1,0:T(2,128)} %bitcast.8, s32[1,1]{1,0:T(1,128)S(6)} %copy.8.count_ref, bf16[94,64,256]{2,1,0:T(8,128)(2,1)} %bitcast.6, bf16[8,64,1536]{2,1,0:T(8,128)(2,1)} %ints_hbm.1), custom_call_target="tpu_custom_call" | custom-call | tf_op jit(solution)/shard_map/pallas_call | solution.py:233
  32.6 1.7 %copy.7 = f32[24,8,256]{2,0,1:T(8,128)} copy(f32[24,8,256]{2,1,0:T(8,128)} %bitcast.7) | data formatting | bytes 393216 | tf_op jit(solution)/shard_map/reshape | solution.py:262

commit v4 on v3

--- a/solution.py
+++ b/solution.py
@@ -1,6 +1,3 @@
-import functools
-import math
-
 import jax
 import jax.numpy as jnp
 from jax import lax
@@ -10,24 +7,9 @@
 
 GROUPS = 12
 LAGS = (1, 5, 9, 13)
-LOW_EXP = -80.0
-
-
-def encode(x, steps):
-    level = jnp.log(jnp.abs(x)) * (steps / math.log(2.0)) + (0.5 - LOW_EXP * steps)
-    level = jnp.maximum(level, 0.0)
-    return jnp.where(x < 0.0, -level, level).astype(jnp.int32).astype(jnp.int16)
-
-
-def decode(code, steps):
-    wide = code.astype(jnp.int32).astype(jnp.float32)
-    size = jnp.exp2(jnp.abs(wide) * (1.0 / steps) + LOW_EXP)
-    value = jnp.where(wide < 0.0, -size, size)
-    return jnp.where(wide == 0.0, 0.0, value)
 
 
 def transform_kernel(
-    steps,
     pairs_ref, count_ref, coeffs_hbm, ints_hbm, out_ref,
     coeffs, ints, turned, left, right, diag,
     own, snd0, rcv0, snd1, rcv1, snd2, rcv2, snd3, rcv3,
@@ -104,17 +86,22 @@
                     source = tile if k % 2 == odd else swap
                     keep = low if k % 2 == 0 else jnp.logical_not(low)
                     diag[odd, k // 4, at_row, at_lane] = jnp.where(keep, source, 0.0).astype(jnp.bfloat16)
-            done = []
-            for odd in range(2):
-                half = jnp.concatenate(
-                    [
-                        jnp.dot(left[part], diag[odd, part], preferred_element_type=jnp.float32).astype(jnp.bfloat16)
-                        for part in range(2)
-                    ],
-                    axis=1,
-                )
-                done.append(jnp.dot(half, right[...], preferred_element_type=jnp.float32).reshape(2, 4, 2, 2, 8, occ))
-            both = jnp.concatenate(done, axis=4)
+            half = jnp.concatenate(
+                [
+                    jnp.concatenate(
+                        [
+                            jnp.dot(left[part], diag[odd, part], preferred_element_type=jnp.float32).astype(jnp.bfloat16)
+                            for part in range(2)
+                        ],
+                        axis=1,
+                    )
+                    for odd in range(2)
+                ],
+                axis=0,
+            )
+            done = jnp.dot(half, right[...], preferred_element_type=jnp.float32)
+            done = done.reshape(2, 2, 4, 2, 2, 8, occ)
+            both = jnp.concatenate([done[0], done[1]], axis=4)
             own[group, :, :, :, step] = both[0]
             snd0[group, :, :, :, step] = both[1].astype(jnp.bfloat16)
             return carry
@@ -157,27 +144,27 @@
     def stage2(group, kind):
         first_copy(group, kind).wait_recv()
         total = chunks(group, kind, slice(None), 1, 0) + rcv1[group, :, 1].astype(jnp.float32)
-        snd2[group] = encode(total, steps)
+        snd2[group] = total.astype(jnp.bfloat16)
         second_copy(group, kind).start()
 
     def gathered(group, kind, z):
         return (
             chunks(group, kind, z, 0, 0)
             + rcv1[group, z, 0].astype(jnp.float32)
-            + decode(rcv2[group, z], steps)
+            + rcv2[group, z].astype(jnp.float32)
         )
 
     def stage3(group, kind):
         second_copy(group, kind).wait_recv()
         for n in (1, 2, 0):
-            snd3[group, n] = encode(gathered(group, kind, n + 1), steps)
+            snd3[group, n] = gathered(group, kind, n + 1).astype(jnp.bfloat16)
             z_copy(group, n).start()
 
     def finish(group, kind):
         total = gathered(group, kind, 0)
         for n in range(3):
             z_copy(group, n).wait_recv()
-        total = total + jnp.sum(decode(rcv3[group], steps), axis=0)
+        total = total + jnp.sum(rcv3[group].astype(jnp.float32), axis=0)
         out_ref[group] = total
 
     stages = (stage1, stage2, stage3, finish)
@@ -224,14 +211,12 @@
     kets = columns // width
     shells = coeffs.shape[0] // width
     per_group = kets // 2 // GROUPS
-    top = math.ceil(math.log2(shell_pairs.shape[0] * width * width * 6 * 0.078125 ** 2)) + 1
-    steps = 32760.0 / (top - LOW_EXP)
     tile = (per_group, 16, occ)
-    bf16, i16 = jnp.bfloat16, jnp.int16
-    hbm = pl.BlockSpec(memory_space=pl.ANY)
+    bf16 = jnp.bfloat16
+    hbm = pl.BlockSpec(memory_space=pltpu.HBM)
     smem = pl.BlockSpec(memory_space=pltpu.SMEM)
     out = pl.pallas_call(
-        functools.partial(transform_kernel, steps),
+        transform_kernel,
         out_shape=jax.ShapeDtypeStruct((GROUPS,) + tile, jnp.float32),
         in_specs=[smem, smem, hbm, hbm],
         out_specs=pl.BlockSpec(memory_space=pltpu.VMEM),
@@ -247,16 +232,16 @@
             pltpu.VMEM((GROUPS, 4, 2, 2) + tile, bf16),
             pltpu.VMEM((GROUPS, 4, 2) + tile, bf16),
             pltpu.VMEM((GROUPS, 4, 2) + tile, bf16),
-            pltpu.VMEM((GROUPS, 4) + tile, i16),
-            pltpu.VMEM((GROUPS, 4) + tile, i16),
-            pltpu.VMEM((GROUPS, 3) + tile, i16),
-            pltpu.VMEM((GROUPS, 3) + tile, i16),
+            pltpu.VMEM((GROUPS, 4) + tile, bf16),
+            pltpu.VMEM((GROUPS, 4) + tile, bf16),
+            pltpu.VMEM((GROUPS, 3) + tile, bf16),
+            pltpu.VMEM((GROUPS, 3) + tile, bf16),
             pltpu.SemaphoreType.DMA((2,)),
             pltpu.SemaphoreType.DMA((GROUPS, 6)),
             pltpu.SemaphoreType.DMA((GROUPS, 6)),
         ],
         compiler_params=pltpu.CompilerParams(
-            collective_id=0, has_side_effects=True, vmem_limit_bytes=60 * 1024 * 1024
+            collective_id=0, has_side_effects=True, vmem_limit_bytes=53 * 1024 * 1024
         ),
     )(shell_pairs.T, block_count, coeffs.reshape(shells, width, occ), integrals)
     return out.reshape(kets, occ // 32, occ).transpose(1, 0, 2)

time: 34.4 us -> 33 us (0.959)
  Pallas kernels: 31.9 us -> 30.7 us
    pallas_call x1, Pallas kernels: 31.9 us -> 30.7 us  [on_device(): pl.pallas_call(transform_kernel, out_shape=jax.ShapeDtypeStruct((GROUPS,)...]
    reshape x1, local copies, waits for them, and re-layouts: 1.67 us -> 0.74 us  [on_device(): return out.reshape(kets, occ // 32, occ).transpose(1, 0, 2)]
    unnamed x0 -> x2, local copies, waits for them, and re-layouts: none -> 0.67 us
where the time goes in v4:
time: 33 us; the launch traced here: 32.8 us
  Pallas kernels  30.7 us (93%)
  local copies, waits for them, and re-layouts  1.41 us (4%)
  between operations  0.67 us (2%)
    pallas_call x1, Pallas kernels, on_device(): pl.pallas_call(transform_kernel, out_shape=jax.ShapeDtypeStruct((GROUPS,)...  30.7 us
    reshape x1, local copies, waits for them, and re-layouts, on_device(): return out.reshape(kets, occ // 32, occ).transpose(1, 0, 2)  0.74 us
    unnamed x2, local copies, waits for them, and re-layouts  0.67 us

profile of v4, /device:TPU:0, one launch (start us, length us, event | category | flops | bytes accessed | tf_op | source)
XLA Modules:
  0.0 32.8 jit_solution(13007267509534902732)
XLA Ops:
  0.7 0.0 copy-start
  0.7 0.7 %copy-done = s32[256,2]{0,1:T(2,128)S(1)} copy-done((s32[256,2]{0,1:T(2,128)S(1)}, s32[256,2]{0,1:T(2,128)}, u32[]{:S(2)}) %copy-start) | copy-done | bytes 2072
  1.3 30.7 %shard_map.46 = f32[12,1,16,256]{3,2,1,0:T(8,128)S(1)} custom-call(s32[2,256]{1,0:T(2,128)S(1)} %bitcast.7, s32[1,1]{1,0:T(1,128)S(6)} %copy.8.count_ref, bf16[94,64,256]{2,1,0:T(8,128)(2,1)} %bitcast.8, bf16[8,64,1536]{2,1,0:T(8,128)(2,1)} %ints_hbm.1), custom_call_target="tpu_custom_call" | custom-call | tf_op jit(solution)/shard_map/pallas_call | solution.py:218
  32.1 0.7 %copy.7 = f32[24,8,256]{2,0,1:T(8,128)} copy(f32[24,8,256]{2,1,0:T(8,128)S(1)} %bitcast.6) | data formatting | bytes 393216 | tf_op jit(solution)/shard_map/reshape | solution.py:247
Async XLA Ops:
  0.7 0.7 %copy-start = (s32[256,2]{0,1:T(2,128)S(1)}, s32[256,2]{0,1:T(2,128)}, u32[]{:S(2)}) copy-start(s32[256,2]{0,1:T(2,128)} %param.6) | copy-start | bytes 6148

commit v5 on v4

--- a/solution.py
+++ b/solution.py
@@ -6,7 +6,7 @@
 from jax.sharding import PartitionSpec as P
 
 GROUPS = 12
-LAGS = (1, 5, 9, 13)
+LAGS = (3, 7, 11, 15)
 
 
 def transform_kernel(

time: 33 us -> 33.7 us (1.021)
  Pallas kernels: 30.7 us -> 31.5 us
    pallas_call x1, Pallas kernels: 30.7 us -> 31.5 us  [on_device(): pl.pallas_call(transform_kernel, out_shape=jax.ShapeDtypeStruct((GROUPS,)...]
where the time goes in v5:
time: 33.7 us; the launch traced here: 33.6 us
  Pallas kernels  31.5 us (93%)
  local copies, waits for them, and re-layouts  1.41 us (4%)
  between operations  0.67 us (2%)
    pallas_call x1, Pallas kernels, on_device(): pl.pallas_call(transform_kernel, out_shape=jax.ShapeDtypeStruct((GROUPS,)...  31.5 us
    reshape x1, local copies, waits for them, and re-layouts, on_device(): return out.reshape(kets, occ // 32, occ).transpose(1, 0, 2)  0.74 us
    unnamed x2, local copies, waits for them, and re-layouts  0.67 us

profile of v5, /device:TPU:0, one launch (start us, length us, event | category | flops | bytes accessed | tf_op | source)
XLA Modules:
  0.0 33.6 jit_solution(4085962546683802696)
XLA Ops:
  0.7 0.0 copy-start
  0.7 0.7 %copy-done = s32[256,2]{0,1:T(2,128)S(1)} copy-done((s32[256,2]{0,1:T(2,128)S(1)}, s32[256,2]{0,1:T(2,128)}, u32[]{:S(2)}) %copy-start) | copy-done | bytes 2072
  1.3 31.5 %shard_map.46 = f32[12,1,16,256]{3,2,1,0:T(8,128)S(1)} custom-call(s32[2,256]{1,0:T(2,128)S(1)} %bitcast.7, s32[1,1]{1,0:T(1,128)S(6)} %copy.8.count_ref, bf16[94,64,256]{2,1,0:T(8,128)(2,1)} %bitcast.8, bf16[8,64,1536]{2,1,0:T(8,128)(2,1)} %ints_hbm.1), custom_call_target="tpu_custom_call" | custom-call | tf_op jit(solution)/shard_map/pallas_call | solution.py:218
  32.8 0.7 %copy.7 = f32[24,8,256]{2,0,1:T(8,128)} copy(f32[24,8,256]{2,1,0:T(8,128)S(1)} %bitcast.6) | data formatting | bytes 393216 | tf_op jit(solution)/shard_map/reshape | solution.py:247
Async XLA Ops:
  0.7 0.7 %copy-start = (s32[256,2]{0,1:T(2,128)S(1)}, s32[256,2]{0,1:T(2,128)}, u32[]{:S(2)}) copy-start(s32[256,2]{0,1:T(2,128)} %param.6) | copy-start | bytes 6148

commit v6 on v5

--- a/solution.py
+++ b/solution.py
@@ -6,6 +6,8 @@
 from jax.sharding import PartitionSpec as P
 
 GROUPS = 12
+COEFF_LOADS = 6
+INT_LOADS = 3
 LAGS = (3, 7, 11, 15)
 
 
@@ -15,10 +17,26 @@
     own, snd0, rcv0, snd1, rcv1, snd2, rcv2, snd3, rcv3,
     load_sem, send_sem, recv_sem,
 ):
-    load_coeffs = pltpu.make_async_copy(coeffs_hbm, coeffs, load_sem.at[0])
-    load_ints = pltpu.make_async_copy(ints_hbm, ints, load_sem.at[1])
-    load_coeffs.start()
-    load_ints.start()
+    shells = coeffs.shape[0]
+    share = -(-shells // COEFF_LOADS)
+    load_coeffs = []
+    for n in range(COEFF_LOADS):
+        part = pl.ds(n * share, min(share, shells - n * share))
+        load_coeffs.append(
+            pltpu.make_async_copy(coeffs_hbm.at[part], coeffs.at[part], load_sem.at[n])
+        )
+    wide = ints.shape[2] // INT_LOADS
+
+    def load_ints(n):
+        part = pl.ds(pl.multiple_of(n * wide, wide), wide)
+        return pltpu.make_async_copy(
+            ints_hbm.at[:, :, part], ints.at[:, :, part], load_sem.at[COEFF_LOADS + n]
+        )
+
+    for item in load_coeffs:
+        item.start()
+    for n in range(INT_LOADS):
+        load_ints(n).start()
 
     me = lax.axis_index("pair")
 
@@ -40,7 +58,8 @@
     occ = coeffs.shape[2]
     span = 4 * width
     diag[...] = jnp.zeros_like(diag)
-    load_coeffs.wait()
+    for item in load_coeffs:
+        item.wait()
     for k in range(slots):
         row_shell = pairs_ref[0, me * slots + k]
         col_shell = pairs_ref[1, me * slots + k]
@@ -67,8 +86,6 @@
             for part in range(2):
                 rows = jnp.concatenate([turned[part, first], turned[part, second]], axis=0)
                 left[part, pl.ds(core * 128 + two * 16, 16), :] = rows.astype(jnp.bfloat16)
-
-    load_ints.wait()
 
     lane = lax.broadcasted_iota(jnp.int32, (width, 2 * width), 1)
     low = lane < width
@@ -175,6 +192,10 @@
 
             @pl.when(tick < GROUPS)
             def _():
+                if kind == 0:
+                    @pl.when(turn % (GROUPS // INT_LOADS // 2) == 0)
+                    def _():
+                        load_ints(turn // (GROUPS // INT_LOADS // 2)).wait()
                 compute(tick)
                 if kind == 0:
                     @pl.when(turn == 0)
@@ -236,7 +257,7 @@
             pltpu.VMEM((GROUPS, 4) + tile, bf16),
             pltpu.VMEM((GROUPS, 3) + tile, bf16),
             pltpu.VMEM((GROUPS, 3) + tile, bf16),
-            pltpu.SemaphoreType.DMA((2,)),
+            pltpu.SemaphoreType.DMA((COEFF_LOADS + INT_LOADS,)),
             pltpu.SemaphoreType.DMA((GROUPS, 6)),
             pltpu.SemaphoreType.DMA((GROUPS, 6)),
         ],

time: 33.7 us -> 33.7 us (level)
  no operation moved by 1% of the time
where the time goes in v6:
time: 33.7 us; the launch traced here: 33.6 us
  Pallas kernels  31.5 us (93%)
  local copies, waits for them, and re-layouts  1.41 us (4%)
  between operations  0.67 us (2%)
    pallas_call x1, Pallas kernels, on_device(): pl.pallas_call(transform_kernel, out_shape=jax.ShapeDtypeStruct((GROUPS,)...  31.5 us
    reshape x1, local copies, waits for them, and re-layouts, on_device(): return out.reshape(kets, occ // 32, occ).transpose(1, 0, 2)  0.74 us
    unnamed x2, local copies, waits for them, and re-layouts  0.67 us

profile of v6, /device:TPU:0, one launch (start us, length us, event | category | flops | bytes accessed | tf_op | source)
XLA Modules:
  0.0 33.6 jit_solution(15347095634097041042)
XLA Ops:
  0.7 0.0 copy-start
  0.7 0.7 %copy-done = s32[256,2]{0,1:T(2,128)S(1)} copy-done((s32[256,2]{0,1:T(2,128)S(1)}, s32[256,2]{0,1:T(2,128)}, u32[]{:S(2)}) %copy-start) | copy-done | bytes 2072
  1.3 31.5 %shard_map.46 = f32[12,1,16,256]{3,2,1,0:T(8,128)S(1)} custom-call(s32[2,256]{1,0:T(2,128)S(1)} %bitcast.7, s32[1,1]{1,0:T(1,128)S(6)} %copy.8.count_ref, bf16[94,64,256]{2,1,0:T(8,128)(2,1)} %bitcast.8, bf16[8,64,1536]{2,1,0:T(8,128)(2,1)} %ints_hbm.1), custom_call_target="tpu_custom_call" | custom-call | tf_op jit(solution)/shard_map/pallas_call | solution.py:239
  32.8 0.7 %copy.7 = f32[24,8,256]{2,0,1:T(8,128)} copy(f32[24,8,256]{2,1,0:T(8,128)S(1)} %bitcast.6) | data formatting | bytes 393216 | tf_op jit(solution)/shard_map/reshape | solution.py:268
Async XLA Ops:
  0.7 0.7 %copy-start = (s32[256,2]{0,1:T(2,128)S(1)}, s32[256,2]{0,1:T(2,128)}, u32[]{:S(2)}) copy-start(s32[256,2]{0,1:T(2,128)} %param.6) | copy-start | bytes 6148

commit v7 on v5

--- a/solution.py
+++ b/solution.py
@@ -11,7 +11,7 @@
 
 def transform_kernel(
     pairs_ref, count_ref, coeffs_hbm, ints_hbm, out_ref,
-    coeffs, ints, turned, left, right, diag,
+    coeffs, ints, turned, left, right, diag, half,
     own, snd0, rcv0, snd1, rcv1, snd2, rcv2, snd3, rcv3,
     load_sem, send_sem, recv_sem,
 ):
@@ -72,41 +72,40 @@
 
     lane = lax.broadcasted_iota(jnp.int32, (width, 2 * width), 1)
     low = lane < width
-    per_group = columns // (2 * width) // GROUPS
-
-    def compute(group):
-        def one_pair(step, carry):
-            cols = pl.ds(pl.multiple_of((group * per_group + step) * 2 * width, 2 * width), 2 * width)
-            for k in range(slots):
-                tile = ints[k, :, cols].astype(jnp.float32)
-                swap = pltpu.roll(tile, width, 1)
-                at_lane = pl.ds((k % 4) // 2 * 2 * width, 2 * width)
-                at_row = pl.ds((k % 4) * width, width)
-                for odd in range(2):
-                    source = tile if k % 2 == odd else swap
-                    keep = low if k % 2 == 0 else jnp.logical_not(low)
-                    diag[odd, k // 4, at_row, at_lane] = jnp.where(keep, source, 0.0).astype(jnp.bfloat16)
-            half = jnp.concatenate(
-                [
-                    jnp.concatenate(
-                        [
-                            jnp.dot(left[part], diag[odd, part], preferred_element_type=jnp.float32).astype(jnp.bfloat16)
-                            for part in range(2)
-                        ],
-                        axis=1,
-                    )
-                    for odd in range(2)
-                ],
-                axis=0,
-            )
-            done = jnp.dot(half, right[...], preferred_element_type=jnp.float32)
-            done = done.reshape(2, 2, 4, 2, 2, 8, occ)
-            both = jnp.concatenate([done[0], done[1]], axis=4)
-            own[group, :, :, :, step] = both[0]
-            snd0[group, :, :, :, step] = both[1].astype(jnp.bfloat16)
-            return carry
-
-        lax.fori_loop(0, per_group, one_pair, 0)
+
+    def lay_out(group, kind):
+        cols = pl.ds(pl.multiple_of(group * 2 * width, 2 * width), 2 * width)
+        for k in range(slots):
+            tile = ints[k, :, cols].astype(jnp.float32)
+            swap = pltpu.roll(tile, width, 1)
+            at_lane = pl.ds((k % 4) // 2 * 2 * width, 2 * width)
+            at_row = pl.ds((k % 4) * width, width)
+            for odd in range(2):
+                source = tile if k % 2 == odd else swap
+                keep = low if k % 2 == 0 else jnp.logical_not(low)
+                diag[kind, odd, k // 4, at_row, at_lane] = jnp.where(keep, source, 0.0).astype(jnp.bfloat16)
+
+    def first_half(kind):
+        for odd in range(2):
+            for part in range(2):
+                product = jnp.dot(left[part], diag[kind, odd, part], preferred_element_type=jnp.float32)
+                half[kind, pl.ds(odd * occ, occ), pl.ds(part * span, span)] = product.astype(jnp.bfloat16)
+
+    def second_half(group, kind):
+        done = jnp.dot(half[kind], right[...], preferred_element_type=jnp.float32)
+        done = done.reshape(2, 2, 4, 2, 2, 8, occ)
+        both = jnp.concatenate([done[0], done[1]], axis=4)
+        own[group] = both[0]
+        snd0[group] = both[1].astype(jnp.bfloat16)
+
+    def compute(group, kind):
+        second_half(group, kind)
+        first_half(1 - kind)
+        lay_out((group + 2) % GROUPS, kind)
+
+    lay_out(0, 0)
+    first_half(0)
+    lay_out(1, 1)
 
     def copy(group, stage, source, target, at):
         return pltpu.make_async_remote_copy(
@@ -175,7 +174,7 @@
 
             @pl.when(tick < GROUPS)
             def _():
-                compute(tick)
+                compute(tick, kind)
                 if kind == 0:
                     @pl.when(turn == 0)
                     def _():
@@ -210,8 +209,7 @@
     occ = coeffs.shape[1]
     kets = columns // width
     shells = coeffs.shape[0] // width
-    per_group = kets // 2 // GROUPS
-    tile = (per_group, 16, occ)
+    tile = (16, occ)
     bf16 = jnp.bfloat16
     hbm = pl.BlockSpec(memory_space=pltpu.HBM)
     smem = pl.BlockSpec(memory_space=pltpu.SMEM)
@@ -226,7 +224,8 @@
             pltpu.VMEM((2, occ // 8, 8, 4 * width), jnp.float32),
             pltpu.VMEM((2, occ, 4 * width), bf16),
             pltpu.VMEM((slots * width, occ), bf16),
-            pltpu.VMEM((2, 2, 4 * width, 4 * width), bf16),
+            pltpu.VMEM((2, 2, 2, 4 * width, 4 * width), bf16),
+            pltpu.VMEM((2, 2 * occ, slots * width), bf16),
             pltpu.VMEM((GROUPS, 4, 2, 2) + tile, jnp.float32),
             pltpu.VMEM((GROUPS, 4, 2, 2) + tile, bf16),
             pltpu.VMEM((GROUPS, 4, 2, 2) + tile, bf16),

time: 33.7 us -> 33.8 us (level)
  no operation moved by 1% of the time
where the time goes in v7:
time: 33.8 us; the launch traced here: 33.7 us
  Pallas kernels  31.6 us (93%)
  local copies, waits for them, and re-layouts  1.41 us (4%)
  between operations  0.67 us (2%)
    pallas_call x1, Pallas kernels, on_device(): pl.pallas_call(transform_kernel, out_shape=jax.ShapeDtypeStruct((GROUPS,)...  31.6 us
    reshape x1, local copies, waits for them, and re-layouts, on_device(): return out.reshape(kets, occ // 32, occ).transpose(1, 0, 2)  0.74 us

profile of v7, /device:TPU:0, one launch (start us, length us, event | category | flops | bytes accessed | tf_op | source)
XLA Modules:
  0.0 33.7 jit_solution(17411268260420631733)
XLA Ops:
  0.7 0.0 copy-start
  0.7 0.7 %copy-done = s32[256,2]{0,1:T(2,128)S(1)} copy-done((s32[256,2]{0,1:T(2,128)S(1)}, s32[256,2]{0,1:T(2,128)}, u32[]{:S(2)}) %copy-start) | copy-done | bytes 2072
  1.3 31.6 %shard_map.46 = f32[12,16,256]{2,1,0:T(8,128)S(1)} custom-call(s32[2,256]{1,0:T(2,128)S(1)} %bitcast.7, s32[1,1]{1,0:T(1,128)S(6)} %copy.8.count_ref, bf16[94,64,256]{2,1,0:T(8,128)(2,1)} %bitcast.8, bf16[8,64,1536]{2,1,0:T(8,128)(2,1)} %ints_hbm.1), custom_call_target="tpu_custom_call" | custom-call | tf_op jit(solution)/shard_map/pallas_call | solution.py:216
  32.9 0.7 %copy.7 = f32[24,8,256]{2,0,1:T(8,128)} copy(f32[24,8,256]{2,1,0:T(8,128)S(1)} %bitcast.6) | data formatting | bytes 393216 | tf_op jit(solution)/shard_map/reshape | solution.py:246
Async XLA Ops:
  0.7 0.7 %copy-start = (s32[256,2]{0,1:T(2,128)S(1)}, s32[256,2]{0,1:T(2,128)}, u32[]{:S(2)}) copy-start(s32[256,2]{0,1:T(2,128)} %param.6) | copy-start | bytes 6148

commit v8 on v7

--- a/solution.py
+++ b/solution.py
@@ -6,7 +6,7 @@
 from jax.sharding import PartitionSpec as P
 
 GROUPS = 12
-LAGS = (3, 7, 11, 15)
+LAGS = (1, 5, 9, 13)
 
 
 def transform_kernel(

time: 33.8 us -> 33.3 us (0.985)
  Pallas kernels: 31.6 us -> 31 us
    pallas_call x1, Pallas kernels: 31.6 us -> 31 us  [on_device(): pl.pallas_call(transform_kernel, out_shape=jax.ShapeDtypeStruct((GROUPS,)...]
where the time goes in v8:
time: 33.3 us; the launch traced here: 33.1 us
  Pallas kernels  31 us (93%)
  local copies, waits for them, and re-layouts  1.41 us (4%)
  between operations  0.67 us (2%)
    pallas_call x1, Pallas kernels, on_device(): pl.pallas_call(transform_kernel, out_shape=jax.ShapeDtypeStruct((GROUPS,)...  31 us
    reshape x1, local copies, waits for them, and re-layouts, on_device(): return out.reshape(kets, occ // 32, occ).transpose(1, 0, 2)  0.74 us
    unnamed x2, local copies, waits for them, and re-layouts  0.67 us

profile of v8, /device:TPU:0, one launch (start us, length us, event | category | flops | bytes accessed | tf_op | source)
XLA Modules:
  0.0 33.1 jit_solution(1467567247918667140)
XLA Ops:
  0.7 0.0 copy-start
  0.7 0.7 %copy-done = s32[256,2]{0,1:T(2,128)S(1)} copy-done((s32[256,2]{0,1:T(2,128)S(1)}, s32[256,2]{0,1:T(2,128)}, u32[]{:S(2)}) %copy-start) | copy-done | bytes 2072
  1.3 31.0 %shard_map.46 = f32[12,16,256]{2,1,0:T(8,128)S(1)} custom-call(s32[2,256]{1,0:T(2,128)S(1)} %bitcast.7, s32[1,1]{1,0:T(1,128)S(6)} %copy.8.count_ref, bf16[94,64,256]{2,1,0:T(8,128)(2,1)} %bitcast.8, bf16[8,64,1536]{2,1,0:T(8,128)(2,1)} %ints_hbm.1), custom_call_target="tpu_custom_call" | custom-call | tf_op jit(solution)/shard_map/pallas_call | solution.py:216
  32.4 0.7 %copy.7 = f32[24,8,256]{2,0,1:T(8,128)} copy(f32[24,8,256]{2,1,0:T(8,128)S(1)} %bitcast.6) | data formatting | bytes 393216 | tf_op jit(solution)/shard_map/reshape | solution.py:246
Async XLA Ops:
  0.7 0.7 %copy-start = (s32[256,2]{0,1:T(2,128)S(1)}, s32[256,2]{0,1:T(2,128)}, u32[]{:S(2)}) copy-start(s32[256,2]{0,1:T(2,128)} %param.6) | copy-start | bytes 6148

commit v9 on v4

--- a/solution.py
+++ b/solution.py
@@ -167,7 +167,8 @@
         total = total + jnp.sum(rcv3[group].astype(jnp.float32), axis=0)
         out_ref[group] = total
 
-    stages = (stage1, stage2, stage3, finish)
+    plan = tuple(zip(LAGS, (stage1, stage2, stage3, finish)))
+    plan = plan[1:] + plan[:1]
 
     def two_ticks(turn, carry):
         for kind in range(2):
@@ -182,7 +183,7 @@
                         pl.semaphore_wait(barrier, len(partners))
                 core_copy(tick).start()
 
-            for lag, stage in zip(LAGS, stages):
+            for lag, stage in plan:
                 group = tick - lag
 
                 @pl.when(jnp.logical_and(group >= 0, group < GROUPS))

time: 33 us -> 33.1 us (level)
  no operation moved by 1% of the time
where the time goes in v9:
time: 33.1 us; the launch traced here: 32.9 us
  Pallas kernels  30.8 us (93%)
  local copies, waits for them, and re-layouts  1.41 us (4%)
  between operations  0.67 us (2%)
    pallas_call x1, Pallas kernels, on_device(): pl.pallas_call(transform_kernel, out_shape=jax.ShapeDtypeStruct((GROUPS,)...  30.8 us
    reshape x1, local copies, waits for them, and re-layouts, on_device(): return out.reshape(kets, occ // 32, occ).transpose(1, 0, 2)  0.74 us
    unnamed x2, local copies, waits for them, and re-layouts  0.67 us

profile of v9, /device:TPU:0, one launch (start us, length us, event | category | flops | bytes accessed | tf_op | source)
XLA Modules:
  0.0 32.9 jit_solution(6365589919241830904)
XLA Ops:
  0.7 0.0 copy-start
  0.7 0.7 %copy-done = s32[256,2]{0,1:T(2,128)S(1)} copy-done((s32[256,2]{0,1:T(2,128)S(1)}, s32[256,2]{0,1:T(2,128)}, u32[]{:S(2)}) %copy-start) | copy-done | bytes 2072
  1.3 30.8 %shard_map.46 = f32[12,1,16,256]{3,2,1,0:T(8,128)S(1)} custom-call(s32[2,256]{1,0:T(2,128)S(1)} %bitcast.7, s32[1,1]{1,0:T(1,128)S(6)} %copy.8.count_ref, bf16[94,64,256]{2,1,0:T(8,128)(2,1)} %bitcast.8, bf16[8,64,1536]{2,1,0:T(8,128)(2,1)} %ints_hbm.1), custom_call_target="tpu_custom_call" | custom-call | tf_op jit(solution)/shard_map/pallas_call | solution.py:219
  32.2 0.7 %copy.7 = f32[24,8,256]{2,0,1:T(8,128)} copy(f32[24,8,256]{2,1,0:T(8,128)S(1)} %bitcast.6) | data formatting | bytes 393216 | tf_op jit(solution)/shard_map/reshape | solution.py:248
Async XLA Ops:
  0.7 0.7 %copy-start = (s32[256,2]{0,1:T(2,128)S(1)}, s32[256,2]{0,1:T(2,128)}, u32[]{:S(2)}) copy-start(s32[256,2]{0,1:T(2,128)} %param.6) | copy-start | bytes 6148
